TPU v7x, 32 devices: a whole 2x2x4 slice. The times are simulated.
32 devices in a mesh: seq: 16 (over z, x, core), head: 2 (over y).
Axes of the slice: x: 2, y: 2, z: 4, core: 2. Of those that a mesh axis runs over, the one named last changes fastest.
Arguments:
- query_tokens: bfloat16 [2, 8192, 1024], P(None, 'seq', 'head'), may hold values from -6 to 6
- key_tokens: bfloat16 [2, 8192, 1024], P(None, 'seq', 'head'), may hold values from -16 to 16
- value_tokens: bfloat16 [2, 8192, 1024], P(None, 'seq', 'head'), may hold values from -16 to 16
- token_rates: float32 [3, 2, 4, 8192], P(None, None, 'head', 'seq'), may hold values from 0.1 to 1
- fast_init: bfloat16 [3, 4, 256, 256], P(None, 'head'), may hold values from -0.375 to 0.375
Outputs:
- mixer_out: bfloat16 [2, 8192, 1024], P(None, ('seq', 'head'))
All inputs are finite; a program needn't handle non-finite values.
Results may differ from a plain program's by a relative error of at most 0.017.
Values may be sent and summed in bfloat16 or wider, within the bound.
A program may use at most 64 MiB of HBM per device.

v0:
```python
import jax
import jax.numpy as jnp
from jax import lax
from jax.sharding import PartitionSpec as P

step_size = 0.05
eps_grad = 1e-05
eps_row = 1e-06


def gradients(current, keys_now, values_now, rate_block):
    rate_cols = jnp.transpose(rate_block, (0, 2, 1))
    gate_proj = jnp.einsum("thd,hde->the", keys_now, current[0], preferred_element_type=jnp.float32)
    up_proj = jnp.einsum("thd,hde->the", keys_now, current[1], preferred_element_type=jnp.float32)
    sigmoid_gate = jax.nn.sigmoid(gate_proj)
    silu_gate = gate_proj * sigmoid_gate
    hidden = (silu_gate * up_proj).astype(jnp.bfloat16)
    scaled_hidden = (hidden.astype(jnp.float32) * rate_cols[2][:, :, None]).astype(jnp.bfloat16)
    grad_down = -jnp.einsum(
        "the,thf->hef", scaled_hidden, values_now, preferred_element_type=jnp.float32
    )
    hidden_grad = -jnp.einsum(
        "thf,hef->the", values_now, current[2], preferred_element_type=jnp.float32
    )
    gate_grad = hidden_grad * up_proj * sigmoid_gate * (1.0 + gate_proj * (1.0 - sigmoid_gate))
    up_grad = hidden_grad * silu_gate
    gate_scaled = (gate_grad * rate_cols[0][:, :, None]).astype(jnp.bfloat16)
    up_scaled = (up_grad * rate_cols[1][:, :, None]).astype(jnp.bfloat16)
    grad_gate = jnp.einsum(
        "thd,the->hde", keys_now, gate_scaled, preferred_element_type=jnp.float32
    )
    grad_up = jnp.einsum("thd,the->hde", keys_now, up_scaled, preferred_element_type=jnp.float32)
    return jnp.stack([grad_gate, grad_up, grad_down])


def renorm(stepped, target):
    return (
        stepped * target * lax.rsqrt(jnp.mean(stepped * stepped, axis=-1, keepdims=True) + eps_row)
    )


def apply_weights(applied, query_now):
    gate_query = jnp.einsum(
        "thd,hde->the", query_now, applied[0], preferred_element_type=jnp.float32
    )
    up_query = jnp.einsum("thd,hde->the", query_now, applied[1], preferred_element_type=jnp.float32)
    hidden_query = (gate_query * jax.nn.sigmoid(gate_query) * up_query).astype(jnp.bfloat16)
    result = jnp.einsum(
        "the,hef->thf", hidden_query, applied[2], preferred_element_type=jnp.float32
    )
    return result.astype(jnp.bfloat16).reshape(result.shape[0], -1)


def body(query_tokens, key_tokens, value_tokens, token_rates, fast_init):
    head_count = fast_init.shape[1]
    head_width = fast_init.shape[2]
    block_count = query_tokens.shape[0]
    tok_rows = query_tokens.shape[1]
    initial = fast_init.astype(jnp.float32)
    target = jnp.sqrt(jnp.mean(initial * initial, axis=-1, keepdims=True))
    fast_state = initial
    current = fast_init
    outputs = []
    for block_index in range(block_count):
        keys_now = key_tokens[block_index].reshape(tok_rows, head_count, head_width)
        values_now = value_tokens[block_index].reshape(tok_rows, head_count, head_width)
        query_now = query_tokens[block_index].reshape(tok_rows, head_count, head_width)
        gradients_now = gradients(current, keys_now, values_now, token_rates[:, block_index])
        summed = lax.psum(gradients_now, "seq")
        grad_rms = jnp.sqrt(jnp.mean(summed * summed, axis=(2, 3), keepdims=True) + eps_grad)
        stepped = fast_state - step_size * summed / grad_rms
        fast_state = renorm(stepped, target)
        current = fast_state.astype(jnp.bfloat16)
        result = apply_weights(current, query_now)
        outputs.append(lax.all_to_all(result, "head", split_axis=0, concat_axis=1, tiled=True))
    return jnp.stack(outputs)


def solution(mesh):
    return jax.shard_map(
        body,
        mesh=mesh,
        in_specs=(
            P(None, "seq", "head"),
            P(None, "seq", "head"),
            P(None, "seq", "head"),
            P(None, None, "head", "seq"),
            P(None, "head", None, None),
        ),
        out_specs=P(None, ("seq", "head"), None),
        check_vma=False,
    )
```

profile of v0, /device:TPU:0, one launch (start us, length us, event | category | flops | bytes accessed | tf_op | source)
XLA Modules:
  0.0 242.4 jit_solution(18098987337632129979)
XLA Ops:
  6.5 1.5 copy.46
  8.4 1.3 convolution_bitcast_fusion.6
  9.6 1.3 convolution_bitcast_fusion.7
  11.2 1.3 fusion.5
  12.6 1.9 fusion.11
  15.6 1.3 pad_maximum_fusion
  17.3 97.7 %all-reduce.3.cloned.1.call-done = f32[3,2,256,256]{2,3,1,0:T(8,128)} async-done(((f32[3,2,256,256]{2,3,1,0:T(8,128)}), f32[3,2,256,256]{2,3,1,0:T(8,128)}) %all-reduce.3.cloned.1.call-update) | async-done | bytes 1572880 | tf_op jit(solution)/shard_map/psum | solution.py:69
  115.0 1.8 multiply_reduce_fusion.3
  120.7 1.2 pad_maximum_fusion.1
  122.0 1.2 copy-done.10
  123.2 1.0 fusion.44
  124.2 2.1 copy.103
  126.3 2.1 copy.106
  128.4 2.3 convolution_bitcast_fusion.5
  130.7 2.9 %fusion.8 = bf16[512,2,256]{0,2,1:T(8,128)(2,1)} fusion(bf16[512,2,256]{0,2,1:T(8,128)(2,1)} %bitcast.159, f32[512,2,256]{0,2,1:T(8,128)} %convolution_bitcast_fusion.5, bf16[3,2,256,256]{2,3,1,0:T(8,128)(2,1)S(1)} %copy-done.3), kind=kOutput, calls=%fused_computation.31 | convolution fusion | flops 270270464 | bytes 2621440 | tf_op jit(solution)/shard_map/the,hef->thf/dot_general | solution.py:48
  133.6 1.2 all_to_all.24
  135.6 3.5 %all-to-all-start = ((bf16[2,256,512]{1,2,0:T(8,128)(2,1)}), bf16[2,256,512]{1,2,0:T(8,128)(2,1)S(1)}, u32[]{:S(2)}, u32[]{:S(2)}) async-start(bf16[2,256,512]{1,2,0:T(8,128)(2,1)} %copy.62), calls=%async_computation | async-start | bytes 1048576 | tf_op jit(solution)/shard_map/all_to_all | solution.py:75
  139.1 77.3 %all-reduce.5.cloned.1.call-done = f32[3,2,256,256]{2,3,1,0:T(8,128)} async-done(((f32[3,2,256,256]{2,3,1,0:T(8,128)}), f32[3,2,256,256]{2,3,1,0:T(8,128)}) %all-reduce.5.cloned.1.call-update) | async-done | bytes 1572880 | tf_op jit(solution)/shard_map/psum | solution.py:69
  216.4 1.8 multiply_reduce_fusion.1
  219.7 0.9 copy-done.5
  220.9 1.7 fusion.9
  223.6 3.5 %all-to-all-start.1 = ((bf16[2,256,512]{1,2,0:T(8,128)(2,1)}), bf16[2,256,512]{1,2,0:T(8,128)(2,1)S(1)}, u32[]{:S(2)}, u32[]{:S(2)}) async-start(bf16[2,256,512]{1,2,0:T(8,128)(2,1)} %copy.77), calls=%async_computation.1 | async-start | bytes 1048576 | tf_op jit(solution)/shard_map/all_to_all | solution.py:75
  227.3 7.0 %all-to-all-done.1 = bf16[2,256,512]{1,2,0:T(8,128)(2,1)S(1)} async-done(((bf16[2,256,512]{1,2,0:T(8,128)(2,1)}), bf16[2,256,512]{1,2,0:T(8,128)(2,1)S(1)}, u32[]{:S(2)}, u32[]{:S(2)}) %all-to-all-start.1) | async-done | bytes 524320 | tf_op jit(solution)/shard_map/all_to_all | solution.py:75
  234.5 1.1 pad_maximum_fusion.2
  (58 shorter events, 10.2 us)
Async XLA Ops:
  6.5 1.5 copy-start.8
  6.5 108.5 %all-reduce.3.cloned.1.call-start = ((), (), s32[]{:S(2)}) async-start(), calls=%async_computation.2 | async-start | bytes 3145728 | tf_op jit(solution)/shard_map/psum | solution.py:69
  8.3 2.5 %copy-start.9 = (bf16[2,512,512]{2,1,0:T(8,128)(2,1)S(1)}, bf16[2,512,512]{2,1,0:T(8,128)(2,1)}, u32[]{:S(2)}) copy-start(bf16[2,512,512]{2,1,0:T(8,128)(2,1)} %param.7) | copy-start | bytes 3145732
  11.0 1.6 copy-start.11
  11.2 1.4 copy-start.6
  12.6 1.9 copy-start.7
  16.8 199.5 %all-reduce.5.cloned.1.call-start = ((), (), s32[]{:S(2)}) async-start(), calls=%async_computation.3 | async-start | bytes 3145728 | tf_op jit(solution)/shard_map/psum | solution.py:69
  115.0 1.9 copy-start
  117.9 0.9 copy-start.2
  122.0 1.2 copy-start.10
  124.2 4.2 %copy-start.3 = (bf16[3,2,256,256]{2,3,1,0:T(8,128)(2,1)S(1)}, bf16[3,2,256,256]{2,3,1,0:T(8,128)(2,1)}, u32[]{:S(2)}) copy-start(bf16[3,2,256,256]{2,3,1,0:T(8,128)(2,1)} %copy-done.2) | copy-start | bytes 2359300
  135.6 88.0 %all-to-all-start = ((bf16[2,256,512]{1,2,0:T(8,128)(2,1)}), bf16[2,256,512]{1,2,0:T(8,128)(2,1)S(1)}, u32[]{:S(2)}, u32[]{:S(2)}) async-start(bf16[2,256,512]{1,2,0:T(8,128)(2,1)} %copy.62), calls=%async_computation | async-start | bytes 1048576 | tf_op jit(solution)/shard_map/all_to_all | solution.py:75
  216.4 1.9 copy-start.1
  218.9 1.6 copy-start.4
  219.7 0.9 copy-start.5
  223.6 10.7 %all-to-all-start.1 = ((bf16[2,256,512]{1,2,0:T(8,128)(2,1)}), bf16[2,256,512]{1,2,0:T(8,128)(2,1)S(1)}, u32[]{:S(2)}, u32[]{:S(2)}) async-start(bf16[2,256,512]{1,2,0:T(8,128)(2,1)} %copy.77), calls=%async_computation.1 | async-start | bytes 1048576 | tf_op jit(solution)/shard_map/all_to_all | solution.py:75
Sparse Core Ops, SparseCore 0:
  16.9 98.0 all-reduce.2
  122.1 94.2 all-reduce.4
where the time goes:
time: 243 us; the launch traced here: 242 us
  waiting for transfers between devices  182 us (75%)
  matrix products  16.5 us (7%)
  local copies, waits for them, and re-layouts  13.7 us (6%)
  between operations  13.7 us (6%)
  other arithmetic  9.48 us (4%)
  starting transfers between devices  7.03 us (3%)
    psum x2, waiting for transfers between devices, body(): summed = lax.psum(gradients_now, 'seq')  175 us
    unnamed x31, local copies, waits for them, and re-layouts  9.11 us
    all_to_all x2, waiting for transfers between devices, body(): lax.all_to_all(result, 'head', split_axis=0, concat_axis=1, tiled=True)  7.03 us
    all_to_all x2, starting transfers between devices, body(): lax.all_to_all(result, 'head', split_axis=0, concat_axis=1, tiled=True)  6.98 us
  transfers between devices with their start and end apart: 4, of which 3 were waited for; matrix products, arithmetic and copies ran while one was open for 7% of the time, Pallas kernels for 0%

commit v1 on v0

v1 whole, which is shorter than its diff:
```python
import functools

import jax
import jax.numpy as jnp
from jax import lax
from jax.experimental import pallas as pl
from jax.experimental.pallas import tpu as pltpu
from jax.sharding import PartitionSpec as P

step_size = 0.05
eps_grad = 1e-05
eps_row = 1e-06
MESH = pl.DeviceIdType.MESH
F32 = jnp.float32
BF16 = jnp.bfloat16


def split_of(n):
    core = 2 if n % 2 == 0 else 1
    chips = n // core
    high = next(f for f in (4, 2, 1) if chips % f == 0)
    return core, chips // high, high


def sigmoid(x):
    return 0.5 * jnp.tanh(0.5 * x) + 0.5


def dot(a, b, ca, cb):
    return lax.dot_general(a, b, (((ca,), (cb,)), ((), ())), preferred_element_type=F32)


def kernel(cfg, q_hbm, k_hbm, v_hbm, rates, w_hbm, out, qb, kb, vb, wb, wf, tgt, rt, ab, bb, gf, gb, s1f, s1b, s2f, s2b,
           ra, rb, rc, ag, ob, load_sem, ss, rs, oss, ors, own_sem):
    blocks, heads, tokens, width, per, tile, ncore, nmid, nhi, nhead = cfg
    chunks = heads // per
    rows = per * 3 * width
    wcol = width // ncore
    me = lax.axis_index("seq")
    y = lax.axis_index("head")
    core = lax.rem(me, ncore)
    chip = lax.div(me, ncore)
    mid = lax.rem(chip, nmid)
    hi = lax.div(chip, nmid)

    def seq_id(c, m, h):
        return {"seq": (h * nmid + m) * ncore + c}

    core_peers = [lax.rem(core + d, ncore) for d in range(1, ncore)]
    mid_peers = [lax.rem(mid + d, nmid) for d in range(1, nmid)]
    hi_peers = [lax.rem(hi + d, nhi) for d in range(1, nhi)]
    head_peers = [lax.rem(y + d, nhead) for d in range(1, nhead)]

    loads = {}

    def load(name, src, dst, index):
        loads[name] = pltpu.make_async_copy(src, dst, load_sem.at[index])
        loads[name].start()

    load("w", w_hbm, wb, 0)
    load(("k", 0), k_hbm.at[0], kb.at[0], 1)
    load(("v", 0), v_hbm.at[0], vb.at[0], 2)
    index = 3
    for b in range(blocks):
        if b:
            load(("k", b), k_hbm.at[b], kb.at[b], index)
            load(("v", b), v_hbm.at[b], vb.at[b], index + 1)
            index += 2
        load(("q", b), q_hbm.at[b], qb.at[b], index)
        index += 1

    barrier = pltpu.get_barrier_semaphore()
    ids = [seq_id(c, mid, hi) for c in core_peers] + [seq_id(core, m, hi) for m in mid_peers]
    ids += [seq_id(core, mid, h) for h in hi_peers] + [{"head": p} for p in head_peers]
    for peer in ids:
        pl.semaphore_signal(barrier, inc=1, device_id=peer, device_id_type=MESH)

    lines = [rates[i, b, h:h + 1, :] for i in range(3) for b in range(blocks) for h in range(heads)]
    pad = rt.shape[1] - len(lines)
    if pad:
        lines.append(jnp.zeros((pad, tokens), F32))
    rt[...] = jnp.transpose(jnp.concatenate(lines, axis=0))

    def rate(i, b, h, at):
        column = (i * blocks + b) * heads + h
        return rt[at, column:column + 1]

    loads["w"].wait()
    for h in range(heads):
        for m in range(3):
            w = wb[m, h].astype(F32)
            tgt[h, m] = jnp.sqrt(jnp.mean(w * w, axis=-1, keepdims=True))
            wf[h, m] = w

    pl.semaphore_wait(barrier, len(ids))

    sends = []

    def send(src, dst, sem, peer):
        copy = pltpu.make_async_remote_copy(src_ref=src, dst_ref=dst, send_sem=ss.at[sem], recv_sem=rs.at[sem],
                                            device_id=peer, device_id_type=MESH)
        copy.start()
        sends.append(copy)
        return copy

    base = {}
    at = 0
    for name, count in (("a", ncore - 1), ("b", nmid - 1), ("c", nhi - 1), ("cc", nhi - 1), ("bb", nmid - 1), ("aa", ncore - 1)):
        base[name] = at
        at += count
    per_chunk = at

    def sem_of(name, b, c, d):
        return (b * chunks + c) * per_chunk + base[name] + d

    def grads(b, h):
        cols = slice(h * width, (h + 1) * width)

        def body(i, carry):
            rows_at = pl.ds(pl.multiple_of(i * tile, tile), tile)
            kt = kb[b, rows_at, cols]
            vt = vb[b, rows_at, cols]
            g = dot(kt, wb[0, h], 1, 0)
            u = dot(kt, wb[1, h], 1, 0)
            e = dot(vt, wb[2, h], 1, 1)
            s = sigmoid(g)
            t = g * s
            hidden = (t * u).astype(BF16).astype(F32)
            ab[rows_at, :] = (hidden * rate(2, b, h, rows_at)).astype(BF16)
            dg = e * u * (s + t * (1.0 - s))
            bb[rows_at, :width] = (dg * rate(0, b, h, rows_at)).astype(BF16)
            bb[rows_at, width:] = (e * t * rate(1, b, h, rows_at)).astype(BF16)
            return carry

        lax.fori_loop(0, tokens // tile, body, 0, unroll=True)
        n13 = dot(kb[b, :, cols], bb[...], 0, 0)
        n2 = dot(ab[...], vb[b, :, cols], 0, 0)
        c, row0 = h // per, (h % per) * 3 * width
        for m, value in enumerate((n13[:, :width], n13[:, width:], n2)):
            for j in range(ncore):
                part = value[:, j * wcol:(j + 1) * wcol]
                put = slice(row0 + m * width, row0 + (m + 1) * width)
                gf[c, j, put, :] = part
                gb[b, c, j, put, :] = part.astype(BF16)

    pending = {}

    def start_a(b, c):
        pending["a", b, c] = [send(gb.at[b, c, p], ra.at[b, c, d], sem_of("a", b, c, d), seq_id(p, mid, hi))
                              for d, p in enumerate(core_peers)]

    def finish(name, b, c):
        for copy in pending.pop((name, b, c)):
            copy.wait_recv()

    def start_b(b, c):
        finish("a", b, c)
        total = gf[c, core]
        for d in range(ncore - 1):
            total = total + ra[b, c, d].astype(F32)
        total = total.reshape(s1f.shape[1:])
        s1f[c] = total
        s1b[b, c] = total.astype(BF16)
        pending["b", b, c] = [send(s1b.at[b, c, p], rb.at[b, c, d], sem_of("b", b, c, d), seq_id(core, p, hi))
                              for d, p in enumerate(mid_peers)]

    def start_c(b, c):
        finish("b", b, c)
        total = s1f[c, mid]
        for d in range(nmid - 1):
            total = total + rb[b, c, d].astype(F32)
        s2f[c] = total
        s2b[b, c] = total.astype(BF16)
        pending["c", b, c] = [send(s2b.at[b, c, p], rc.at[b, c, d], sem_of("c", b, c, d), seq_id(core, mid, p))
                              for d, p in enumerate(hi_peers)]

    def start_cc(b, c):
        finish("c", b, c)
        total = s2f[c, hi]
        for d in range(nhi - 1):
            total = total + rc[b, c, d].astype(F32)
        ag[b, c, core, mid, hi] = total.astype(BF16)
        part = ag.at[b, c, core, mid, hi]
        pending["cc", b, c] = [send(part, part, sem_of("cc", b, c, d), seq_id(core, mid, p))
                               for d, p in enumerate(hi_peers)]

    def start_bb(b, c):
        finish("cc", b, c)
        part = ag.at[b, c, core, mid]
        pending["bb", b, c] = [send(part, part, sem_of("bb", b, c, d), seq_id(core, p, hi))
                               for d, p in enumerate(mid_peers)]

    def start_aa(b, c):
        finish("bb", b, c)
        part = ag.at[b, c, core]
        pending["aa", b, c] = [send(part, part, sem_of("aa", b, c, d), seq_id(p, mid, hi))
                               for d, p in enumerate(core_peers)]

    def update(b, c):
        finish("aa", b, c)
        halves = [ag[b, c, j].reshape(rows, wcol) for j in range(ncore)]
        for p in range(per):
            h = c * per + p
            for m in range(3):
                row0 = (p * 3 + m) * width
                n = jnp.concatenate([x[row0:row0 + width].astype(F32) for x in halves], axis=1)
                mean = jnp.sum(jnp.sum(n * n, axis=0, keepdims=True), axis=1, keepdims=True) * (1.0 / (width * width))
                stepped = wf[h, m] + n * (step_size * lax.rsqrt(mean + eps_grad))
                scale = tgt[h, m] * lax.rsqrt(jnp.mean(stepped * stepped, axis=-1, keepdims=True) + eps_row)
                new = stepped * scale
                wf[h, m] = new
                wb[m, h] = new.astype(BF16)

    out_copies = []
    own_copies = []
    part_tokens = tokens // nhead

    def apply(b, h):
        cols = slice(h * width, (h + 1) * width)
        x = qb[b, :, cols]
        g = dot(x, wb[0, h], 1, 0)
        u = dot(x, wb[1, h], 1, 0)
        hq = (g * sigmoid(g) * u).astype(BF16)
        result = dot(hq, wb[2, h], 1, 0).astype(BF16)
        ob[b, h] = result.reshape(nhead, part_tokens, width)
        target = out.at[b, :, pl.ds(pl.multiple_of((y * heads + h) * width, width), width)]
        for d, p in enumerate(head_peers):
            sem = (b * heads + h) * (nhead - 1) + d
            copy = pltpu.make_async_remote_copy(src_ref=ob.at[b, h, p], dst_ref=target, send_sem=oss.at[sem],
                                                recv_sem=ors.at[sem], device_id={"head": p}, device_id_type=MESH)
            copy.start()
            out_copies.append(copy)
        copy = pltpu.make_async_copy(ob.at[b, h, y], target, own_sem.at[b * heads + h])
        copy.start()
        own_copies.append(copy)

    def chunk_heads(c):
        return range(c * per, (c + 1) * per)

    loads["k", 0].wait()
    loads["v", 0].wait()
    for c in range(chunks):
        for h in chunk_heads(c):
            grads(0, h)
        start_a(0, c)
    for b in range(blocks):
        for c in range(chunks):
            start_b(b, c)
        if b:
            for h in range(heads):
                apply(b - 1, h)
        for step in (start_c, start_cc, start_bb, start_aa):
            for c in range(chunks):
                step(b, c)
        loads["q", b].wait()
        if b < blocks - 1:
            loads["k", b + 1].wait()
            loads["v", b + 1].wait()
        for c in range(chunks):
            update(b, c)
            for h in chunk_heads(c):
                if b < blocks - 1:
                    grads(b + 1, h)
                else:
                    apply(b, h)
            if b < blocks - 1:
                start_a(b + 1, c)

    for copy in out_copies:
        copy.wait_recv()
    for copy in own_copies:
        copy.wait()
    for copy in sends + out_copies:
        copy.wait_send()


def solution(mesh):
    nseq, nhead = mesh.shape["seq"], mesh.shape["head"]
    ncore, nmid, nhi = split_of(nseq)

    def body(q, k, v, rates, w):
        blocks, tokens, _ = q.shape
        heads, width = w.shape[1], w.shape[2]
        share = nmid * nhi
        per = next(p for p in range(1, heads + 1) if heads % p == 0 and ((p * 3 * width) % (16 * share) == 0 or p == heads))
        chunks = heads // per
        rows = per * 3 * width
        piece = rows // share
        wcol = width // ncore
        tile = 128 if tokens % 128 == 0 else tokens
        rate_cols = -(-3 * blocks * heads // 8) * 8
        copies = (ncore - 1) + (nmid - 1) + (nhi - 1)
        cfg = (blocks, heads, tokens, width, per, tile, ncore, nmid, nhi, nhead)
        vmem = pltpu.VMEM
        dma = pltpu.SemaphoreType.DMA
        scratch = [
            vmem(q.shape, BF16), vmem(k.shape, BF16), vmem(v.shape, BF16),
            vmem(w.shape, BF16),
            vmem((heads, 3, width, width), F32),
            vmem((heads, 3, width, 1), F32),
            vmem((tokens, rate_cols), F32),
            vmem((tokens, width), BF16),
            vmem((tokens, 2 * width), BF16),
            vmem((chunks, ncore, rows, wcol), F32),
            vmem((blocks, chunks, ncore, rows, wcol), BF16),
            vmem((chunks, nmid, nhi, piece, wcol), F32),
            vmem((blocks, chunks, nmid, nhi, piece, wcol), BF16),
            vmem((chunks, nhi, piece, wcol), F32),
            vmem((blocks, chunks, nhi, piece, wcol), BF16),
            vmem((blocks, chunks, max(ncore - 1, 1), rows, wcol), BF16),
            vmem((blocks, chunks, max(nmid - 1, 1), nhi, piece, wcol), BF16),
            vmem((blocks, chunks, max(nhi - 1, 1), piece, wcol), BF16),
            vmem((blocks, chunks, ncore, nmid, nhi, piece, wcol), BF16),
            vmem((blocks, heads, nhead, tokens // nhead, width), BF16),
            dma((1 + 3 * blocks,)),
            dma((blocks * chunks * 2 * copies,)), dma((blocks * chunks * 2 * copies,)),
            dma((blocks * heads * max(nhead - 1, 1),)), dma((blocks * heads * max(nhead - 1, 1),)),
            dma((blocks * heads,)),
        ]
        anywhere = pl.BlockSpec(memory_space=pl.ANY)
        return pl.pallas_call(
            functools.partial(kernel, cfg),
            out_shape=jax.ShapeDtypeStruct((blocks, tokens // nhead, nhead * heads * width), BF16),
            in_specs=[anywhere, anywhere, anywhere, pl.BlockSpec(memory_space=pltpu.VMEM), anywhere],
            out_specs=anywhere,
            scratch_shapes=scratch,
            compiler_params=pltpu.CompilerParams(collective_id=0, has_side_effects=True,
                                                 vmem_limit_bytes=44 * 1024 * 1024),
        )(q, k, v, rates, w)

    return jax.shard_map(
        body,
        mesh=mesh,
        in_specs=(
            P(None, "seq", "head"),
            P(None, "seq", "head"),
            P(None, "seq", "head"),
            P(None, None, "head", "seq"),
            P(None, "head", None, None),
        ),
        out_specs=P(None, ("seq", "head"), None),
        check_vma=False,
    )
```

time: 243 us -> 64.2 us (0.26)
  waiting for transfers between devices: 182 us -> 0 us
  Pallas kernels: 0 us -> 57.4 us
  matrix products: 16.5 us -> 0 us
  between operations: 13.7 us -> 0.01 us
  other arithmetic: 9.48 us -> 0 us
  local copies, waits for them, and re-layouts: 13.7 us -> 6.51 us
  starting transfers between devices: 7.03 us -> 0 us
    psum x2 -> x0, waiting for transfers between devices: 175 us -> none  [body(): summed = lax.psum(gradients_now, 'seq')]
    pallas_call x0 -> x1, Pallas kernels: none -> 57.4 us  [body(): pl.pallas_call(functools.partial(kernel, cfg), out_shape=jax.ShapeDtypeSt...]
    dot_general x16 -> x0, matrix products: 16.5 us -> none  [the longest x2 4.54 us: apply_weights(): jnp.einsum('the,hef->thf', hidden_query, applied[2], preferred_element_ty...]
    all_to_all x2 -> x0, waiting for transfers between devices: 7.03 us -> none  [body(): lax.all_to_all(result, 'head', split_axis=0, concat_axis=1, tiled=True)]
    all_to_all x2 -> x0, starting transfers between devices: 6.98 us -> none  [body(): lax.all_to_all(result, 'head', split_axis=0, concat_axis=1, tiled=True)]
    reduce_sum x4 -> x0, other arithmetic: 4.65 us -> none  [the longest x2 3.51 us: body(): jnp.mean(summed * summed, axis=(2, 3), keepdims=True) + eps_grad]
    another operation x3 -> x0, other arithmetic: 3.56 us -> none  [the longest x2 2.5 us: gradients(): return jnp.stack([grad_gate, grad_up, grad_down])]
    all_to_all x4 -> x0, local copies, waits for them, and re-layouts: 3.01 us -> none  [body(): lax.all_to_all(result, 'head', split_axis=0, concat_axis=1, tiled=True)]
  transfers between devices with their start and end apart: 4 -> 0, of which waited for: 3 -> 0; matrix products, arithmetic and copies ran while one was open for 7% -> 0% of each run, Pallas kernels for 0% -> 0%
where the time goes in v1:
time: 64.2 us; the launch traced here: 63.9 us
  Pallas kernels  57.4 us (89%)
  local copies, waits for them, and re-layouts  6.51 us (10%)
    pallas_call x1, Pallas kernels, body(): pl.pallas_call(functools.partial(kernel, cfg), out_shape=jax.ShapeDtypeSt...  57.4 us
    unnamed x11, local copies, waits for them, and re-layouts  6.51 us

profile of v1, /device:TPU:0, one launch (start us, length us, event | category | flops | bytes accessed | tf_op | source)
XLA Modules:
  0.0 63.9 jit_solution(4886752606152409645)
XLA Ops:
  0.0 0.0 copy-start
  0.0 1.2 %copy-done = bf16[2,512,512]{2,1,0:T(8,128)(2,1)S(1)} copy-done((bf16[2,512,512]{2,1,0:T(8,128)(2,1)S(1)}, bf16[2,512,512]{2,1,0:T(8,128)(2,1)}, u32[]{:S(2)}) %copy-start) | copy-done | bytes 1048600
  1.2 0.0 copy-start.1
  1.2 1.2 %copy-done.1 = bf16[2,512,512]{2,1,0:T(8,128)(2,1)S(1)} copy-done((bf16[2,512,512]{2,1,0:T(8,128)(2,1)S(1)}, bf16[2,512,512]{2,1,0:T(8,128)(2,1)}, u32[]{:S(2)}) %copy-start.1) | copy-done | bytes 1048600
  2.5 0.0 copy-start.2
  2.5 1.2 %copy-done.2 = bf16[2,512,512]{2,1,0:T(8,128)(2,1)S(1)} copy-done((bf16[2,512,512]{2,1,0:T(8,128)(2,1)S(1)}, bf16[2,512,512]{2,1,0:T(8,128)(2,1)}, u32[]{:S(2)}) %copy-start.2) | copy-done | bytes 1048600
  3.7 0.0 copy-start.3
  3.7 1.1 %copy-done.3 = bf16[3,2,256,256]{3,2,1,0:T(8,128)(2,1)S(1)} copy-done((bf16[3,2,256,256]{3,2,1,0:T(8,128)(2,1)S(1)}, bf16[3,2,256,256]{3,2,1,0:T(8,128)(2,1)}, u32[]{:S(2)}) %copy-start.3) | copy-done | bytes 786456
  4.8 0.0 copy-start.4
  4.8 0.7 %copy-done.4 = f32[3,2,2,512]{3,2,1,0:T(2,128)S(1)} copy-done((f32[3,2,2,512]{3,2,1,0:T(2,128)S(1)}, f32[3,2,2,512]{3,2,1,0:T(2,128)}, u32[]{:S(2)}) %copy-start.4) | copy-done | bytes 24600
  5.5 57.4 %shard_map.55 = bf16[2,256,1024]{2,1,0:T(8,128)(2,1)S(1)} custom-call(bf16[2,512,512]{2,1,0:T(8,128)(2,1)S(1)} %copy-done, bf16[2,512,512]{2,1,0:T(8,128)(2,1)S(1)} %copy-done.1, bf16[2,512,512]{2,1,0:T(8,128)(2,1)S(1)} %copy-done.2, f32[3,2,2,512]{3,2,1,0:T(2,128)S(1)} %copy-done.4, bf16[3,2,256,256]{3,2,1,0:T(8,128)(2,1)S(1)} %copy-done.3), custom_call_target="tpu_custom_call" | custom-call | tf_op jit(solution)/shard_map/pallas_call | solution.py:321
  62.9 1.0 %copy.7 = bf16[2,256,1024]{2,1,0:T(8,128)(2,1)} copy(bf16[2,256,1024]{2,1,0:T(8,128)(2,1)S(1)} %shard_map.55) | data formatting | bytes 2097152
Async XLA Ops:
  0.0 1.2 %copy-start = (bf16[2,512,512]{2,1,0:T(8,128)(2,1)S(1)}, bf16[2,512,512]{2,1,0:T(8,128)(2,1)}, u32[]{:S(2)}) copy-start(bf16[2,512,512]{2,1,0:T(8,128)(2,1)} %q_hbm.1) | copy-start | bytes 3145732
  1.2 1.2 %copy-start.1 = (bf16[2,512,512]{2,1,0:T(8,128)(2,1)S(1)}, bf16[2,512,512]{2,1,0:T(8,128)(2,1)}, u32[]{:S(2)}) copy-start(bf16[2,512,512]{2,1,0:T(8,128)(2,1)} %k_hbm.1) | copy-start | bytes 3145732
  2.5 1.2 %copy-start.2 = (bf16[2,512,512]{2,1,0:T(8,128)(2,1)S(1)}, bf16[2,512,512]{2,1,0:T(8,128)(2,1)}, u32[]{:S(2)}) copy-start(bf16[2,512,512]{2,1,0:T(8,128)(2,1)} %v_hbm.1) | copy-start | bytes 3145732
  3.7 1.1 %copy-start.3 = (bf16[3,2,256,256]{3,2,1,0:T(8,128)(2,1)S(1)}, bf16[3,2,256,256]{3,2,1,0:T(8,128)(2,1)}, u32[]{:S(2)}) copy-start(bf16[3,2,256,256]{3,2,1,0:T(8,128)(2,1)} %w_hbm.1) | copy-start | bytes 2359300
  4.8 0.7 %copy-start.4 = (f32[3,2,2,512]{3,2,1,0:T(2,128)S(1)}, f32[3,2,2,512]{3,2,1,0:T(2,128)}, u32[]{:S(2)}) copy-start(f32[3,2,2,512]{3,2,1,0:T(2,128)} %rates.1) | copy-start | bytes 73732

commit v2 on v0

v2 whole, which is shorter than its diff:
```python
import functools
import math

import jax
import jax.numpy as jnp
from jax import lax
from jax.experimental import pallas as pl
from jax.experimental.pallas import tpu as pltpu
from jax.sharding import PartitionSpec as P

step_size = 0.05
eps_grad = 1e-05
eps_row = 1e-06
lanes = 128
MESH = pl.DeviceIdType.MESH
F32 = jnp.float32
BF16 = jnp.bfloat16


def split_of(n, heads):
    core = math.gcd(2, math.gcd(n, heads))
    chips = n // core
    high = next(f for f in (4, 2, 1) if chips % f == 0)
    return core, chips // high, high


def sigmoid(x):
    return 0.5 * jnp.tanh(0.5 * x) + 0.5


def dot(a, b, ca, cb):
    return lax.dot_general(a, b, (((ca,), (cb,)), ((), ())), preferred_element_type=F32)


def kernel(cfg, q_hbm, k_hbm, v_hbm, rates, w_hbm, out, qb, kb, vb, wb, wf, tgt, lb, lr, rt, ab, bb, ob, load_sem, xs, xr, ss, rs,
           oss, ors, own_sem, *chunk_refs):
    blocks, heads, tokens, width, tile, ncore, nmid, nhi, nhead = cfg
    own = heads // ncore
    folds = width // lanes
    me = lax.axis_index("seq")
    y = lax.axis_index("head")
    core = lax.rem(me, ncore)
    chip = lax.div(me, ncore)
    mid = lax.rem(chip, nmid)
    hi = lax.div(chip, nmid)

    def seq_of(c, m, h):
        return (h * nmid + m) * ncore + c

    core_peers = [lax.rem(core + d, ncore) for d in range(1, ncore)]
    mid_peers = [lax.rem(mid + d, nmid) for d in range(1, nmid)]
    hi_peers = [lax.rem(hi + d, nhi) for d in range(1, nhi)]
    out_peers = [(lax.rem(core + dc, ncore), lax.rem(y + dy, nhead)) for dy in range(nhead) for dc in range(ncore) if dc or dy]
    order = list(range(ncore - 1, len(out_peers))) + list(range(ncore - 1))

    def mid_id(p):
        return {"seq": seq_of(core, p, hi)}

    def hi_id(p):
        return {"seq": seq_of(core, mid, p)}

    def out_id(p):
        return {"seq": seq_of(p[0], mid, hi), "head": p[1]}

    barrier = pltpu.get_barrier_semaphore()
    ids = [out_id(p) for p in out_peers] + [mid_id(p) for p in mid_peers] + [hi_id(p) for p in hi_peers]
    for peer in ids:
        pl.semaphore_signal(barrier, inc=1, device_id=peer, device_id_type=MESH)

    loads = {}

    def head_cols(c):
        return pl.ds(pl.multiple_of(c * (own * width), lanes), own * width)

    loads["w"] = pltpu.make_async_copy(w_hbm.at[:, pl.ds(core * own, own)], wb, load_sem.at[0])
    loads["w"].start()
    arrays = {"k": (k_hbm, kb), "v": (v_hbm, vb), "q": (q_hbm, qb)}
    names = [("k", 0), ("v", 0)]
    for b in range(blocks):
        names += [("k", b + 1), ("v", b + 1), ("q", b)] if b < blocks - 1 else [("q", b)]
    for i, (name, b) in enumerate(names):
        src, dst = arrays[name]
        loads[name, b] = pltpu.make_async_copy(src.at[b, :, head_cols(core)], dst.at[b, core], load_sem.at[1 + i])
        loads[name, b].start()

    count = 3 * blocks * own
    for dc in range(ncore):
        c = lax.rem(core + dc, ncore)
        lines = [rates[i, b, pl.ds(c * own + h, 1), :] for i in range(3) for b in range(blocks) for h in range(own)]
        if lb.shape[1] > count:
            lines.append(jnp.zeros((lb.shape[1] - count, tokens), F32))
        lb[dc] = jnp.concatenate(lines, axis=0)

    pl.semaphore_wait(barrier, len(ids))

    sends = []
    gifts = {}

    def gift(key, src, dst, p, sem):
        copy = pltpu.make_async_remote_copy(src_ref=src, dst_ref=dst, send_sem=xs.at[sem], recv_sem=xr.at[sem],
                                            device_id={"seq": seq_of(p, mid, hi)}, device_id_type=MESH)
        copy.start()
        sends.append(copy)
        gifts.setdefault(key, []).append(copy)

    for d, p in enumerate(core_peers):
        first = d * (1 + len(names))
        gift("rates", lb.at[d + 1], lr.at[d], p, first)
        for i, (name, b) in enumerate(names):
            src, dst = arrays[name]
            gift((name, b), src.at[b, :, head_cols(p)], dst.at[b, core], p, first + 1 + i)

    rt[core] = jnp.transpose(lb[0])
    loads["w"].wait()
    for h in range(own):
        for m in range(3):
            w = wb[m, h].astype(F32)
            tgt[h, m] = jnp.sqrt(jnp.mean(w * w, axis=-1, keepdims=True))
            wf[h, m] = w

    def arrived(key):
        for copy in gifts.get(key, ()):
            copy.wait_recv()

    per_chunk = 2 * (nmid - 1 + nhi - 1)
    refs = {}
    for b in range(blocks):
        for h in range(own):
            for m in range(3):
                i = (h * 3 + m) * 7
                refs[b, h, m] = [r.at[b] for r in chunk_refs[i:i + 7]]

    def sides(m):
        one, two = (nmid, mid, mid_peers, mid_id), (nhi, hi, hi_peers, hi_id)
        return (one, two) if m < 2 else (two, one)

    pending = {}

    def exchange(key, number, pairs, peers, id_of):
        b, h, m = key
        copies = []
        for d, p in enumerate(peers):
            src, dst = pairs(d, p)
            sem = ((b * own + h) * 3 + m) * per_chunk + number + d
            copy = pltpu.make_async_remote_copy(src_ref=src, dst_ref=dst, send_sem=ss.at[sem], recv_sem=rs.at[sem],
                                                device_id=id_of(p), device_id_type=MESH)
            copy.start()
            copies.append(copy)
        sends.extend(copies)
        pending[key] = copies

    def finish(key):
        for copy in pending.pop(key):
            copy.wait_recv()

    def start_first(key, value):
        gf, gb, r1, sf, sb, r2, ag = refs[key]
        (n1, _, peers, id_of), _ = sides(key[2])
        folded = jnp.concatenate([value[:, j * lanes:(j + 1) * lanes] for j in range(folds)], axis=0).reshape(gf.shape)
        gf[...] = folded
        gb[...] = folded.astype(BF16)
        exchange(key, 0, lambda d, p: (gb.at[p], r1.at[d]), peers, id_of)

    def start_second(key):
        finish(key)
        gf, gb, r1, sf, sb, r2, ag = refs[key]
        (n1, my1, peers1, _), (n2, my2, peers, id_of) = sides(key[2])
        total = gf[my1]
        for d in range(n1 - 1):
            total = total + r1[d].astype(F32)
        sf[...] = total
        sb[...] = total.astype(BF16)
        exchange(key, n1 - 1, lambda d, p: (sb.at[p], r2.at[d]), peers, id_of)

    def start_third(key):
        finish(key)
        gf, gb, r1, sf, sb, r2, ag = refs[key]
        (n1, my1, _, _), (n2, my2, peers, id_of) = sides(key[2])
        total = sf[my2]
        for d in range(n2 - 1):
            total = total + r2[d].astype(F32)
        ag[my1, my2] = total.astype(BF16)
        part = ag.at[my1, my2]
        exchange(key, n1 + n2 - 2, lambda d, p: (part, part), peers, id_of)

    def start_fourth(key):
        finish(key)
        ag = refs[key][6]
        (n1, my1, peers, id_of), (n2, _, _, _) = sides(key[2])
        part = ag.at[my1]
        exchange(key, n1 + 2 * n2 - 3, lambda d, p: (part, part), peers, id_of)

    def update(key):
        finish(key)
        b, h, m = key
        x = refs[key][6][...].reshape(folds * width, lanes)
        n = jnp.concatenate([x[j * width:(j + 1) * width].astype(F32) for j in range(folds)], axis=1)
        mean = jnp.sum(jnp.sum(n * n, axis=0, keepdims=True), axis=1, keepdims=True) * (1.0 / (width * width))
        stepped = wf[h, m] + n * (step_size * lax.rsqrt(mean + eps_grad))
        new = stepped * (tgt[h, m] * lax.rsqrt(jnp.mean(stepped * stepped, axis=-1, keepdims=True) + eps_row))
        wf[h, m] = new
        wb[m, h] = new.astype(BF16)

    def grads(b, h):
        cols = slice(h * width, (h + 1) * width)

        def part(c):
            def body(i, carry):
                at = pl.ds(pl.multiple_of(i * tile, tile), tile)
                kt = kb[b, c, at, cols]
                vt = vb[b, c, at, cols]
                g = dot(kt, wb[0, h], 1, 0)
                u = dot(kt, wb[1, h], 1, 0)
                e = dot(vt, wb[2, h], 1, 1)

                def rate(i):
                    column = (i * blocks + b) * own + h
                    return rt[c, at, column:column + 1]

                s = sigmoid(g)
                t = g * s
                hidden = (t * u).astype(BF16).astype(F32)
                ab[c, at, :] = (hidden * rate(2)).astype(BF16)
                dg = e * u * (s + t * (1.0 - s))
                bb[c, at, :width] = (dg * rate(0)).astype(BF16)
                bb[c, at, width:] = (e * t * rate(1)).astype(BF16)
                return carry

            lax.fori_loop(0, tokens // tile, body, 0, unroll=True)

        if h == 0:
            loads["k", b].wait()
            loads["v", b].wait()
        part(core)
        for d, p in enumerate(core_peers):
            if h == 0 and d == 0:
                arrived(("k", b))
                arrived(("v", b))
                if b == 0:
                    arrived("rates")
                    for e, other in enumerate(core_peers):
                        rt[lax.rem(core + ncore - 1 - e, ncore)] = jnp.transpose(lr[e])
            part(p)
        flat = ncore * tokens
        start_first((b, h, 2), dot(ab[...].reshape(flat, width), vb[b, :, :, cols].reshape(flat, width), 0, 0))
        n13 = dot(kb[b, :, :, cols].reshape(flat, width), bb[...].reshape(flat, 2 * width), 0, 0)
        start_first((b, h, 0), n13[:, :width])
        start_first((b, h, 1), n13[:, width:])

    part_tokens = tokens // nhead
    out_copies = []
    own_copies = []

    def apply(b):
        loads["q", b].wait()
        arrived(("q", b))
        target = out.at[b, :, pl.ds(pl.multiple_of((y * heads + core * own) * width, lanes), own * width)]

        def rows_of(c, part):
            at = pl.ds(pl.multiple_of(part * part_tokens, part_tokens), part_tokens)
            for h in range(own):
                cols = slice(h * width, (h + 1) * width)
                x = qb[b, c, at, cols]
                g = dot(x, wb[0, h], 1, 0)
                u = dot(x, wb[1, h], 1, 0)
                hq = (g * sigmoid(g) * u).astype(BF16)
                ob[b, c, part, :, cols] = dot(hq, wb[2, h], 1, 0).astype(BF16)

        for d in order:
            p = out_peers[d]
            rows_of(*p)
            sem = b * len(out_peers) + d
            copy = pltpu.make_async_remote_copy(src_ref=ob.at[b, p[0], p[1]], dst_ref=target, send_sem=oss.at[sem],
                                                recv_sem=ors.at[sem], device_id=out_id(p), device_id_type=MESH)
            copy.start()
            out_copies.append(copy)
        rows_of(core, y)
        copy = pltpu.make_async_copy(ob.at[b, core, y], target, own_sem.at[b])
        copy.start()
        own_copies.append(copy)

    for h in range(own):
        grads(0, h)
    for b in range(blocks):
        turn = (2, 0, 1)
        keys = [(b, h, m) for h in range(own) for m in turn]
        for key in keys:
            start_second(key)
        if b:
            apply(b - 1)
        for step in (start_third, start_fourth):
            for key in keys:
                step(key)
        if b < blocks - 1:
            for h in range(own):
                for m in turn:
                    update((b, h, m))
                grads(b + 1, h)
        else:
            for key in keys:
                update(key)
            apply(b)

    for copy in out_copies:
        copy.wait_recv()
    for copy in own_copies:
        copy.wait()
    for copy in sends + out_copies:
        copy.wait_send()


def solution(mesh):
    nseq, nhead = mesh.shape["seq"], mesh.shape["head"]

    def body(q, k, v, rates, w):
        blocks, tokens, _ = q.shape
        heads, width = w.shape[1], w.shape[2]
        ncore, nmid, nhi = split_of(nseq, heads)
        own = heads // ncore
        tile = 128 if tokens % 128 == 0 else tokens
        cfg = (blocks, heads, tokens, width, tile, ncore, nmid, nhi, nhead)
        vmem = pltpu.VMEM
        dma = pltpu.SemaphoreType.DMA
        loads = 3 * blocks
        others = max(ncore - 1, 1)
        lines = -(-3 * blocks * own // 8) * 8
        copies = blocks * own * 3 * 2 * (nmid - 1 + nhi - 1)
        out_copies = blocks * (ncore * nhead - 1)
        scratch = [
            *[vmem((blocks, ncore, tokens, own * width), BF16)] * 3,
            vmem((3, own, width, width), BF16),
            vmem((own, 3, width, width), F32),
            vmem((own, 3, width, 1), F32),
            vmem((ncore, lines, tokens), F32),
            vmem((others, lines, tokens), F32),
            vmem((ncore, tokens, lines), F32),
            vmem((ncore, tokens, width), BF16),
            vmem((ncore, tokens, 2 * width), BF16),
            vmem((blocks, ncore, nhead, tokens // nhead, own * width), BF16),
            dma((1 + loads,)),
            *[dma((others * (1 + loads),))] * 2,
            *[dma((copies,))] * 2,
            *[dma((out_copies,))] * 2,
            dma((blocks,)),
        ]
        piece = width * width // lanes // (nmid * nhi)
        for _ in range(own):
            for m in range(3):
                n1, n2 = (nmid, nhi) if m < 2 else (nhi, nmid)
                scratch += [
                    vmem((blocks, n1, n2, piece, lanes), F32),
                    vmem((blocks, n1, n2, piece, lanes), BF16),
                    vmem((blocks, max(n1 - 1, 1), n2, piece, lanes), BF16),
                    vmem((blocks, n2, piece, lanes), F32),
                    vmem((blocks, n2, piece, lanes), BF16),
                    vmem((blocks, max(n2 - 1, 1), piece, lanes), BF16),
                    vmem((blocks, n1, n2, piece, lanes), BF16),
                ]
        anywhere = pl.BlockSpec(memory_space=pl.ANY)
        return pl.pallas_call(
            functools.partial(kernel, cfg),
            out_shape=jax.ShapeDtypeStruct((blocks, tokens // nhead, nhead * heads * width), BF16),
            in_specs=[anywhere, anywhere, anywhere, pl.BlockSpec(memory_space=pltpu.VMEM), anywhere],
            out_specs=anywhere,
            scratch_shapes=scratch,
            compiler_params=pltpu.CompilerParams(collective_id=0, has_side_effects=True,
                                                 vmem_limit_bytes=62 * 1024 * 1024),
        )(q, k, v, rates, w)

    return jax.shard_map(
        body,
        mesh=mesh,
        in_specs=(
            P(None, "seq", "head"),
            P(None, "seq", "head"),
            P(None, "seq", "head"),
            P(None, None, "head", "seq"),
            P(None, "head", None, None),
        ),
        out_specs=P(None, ("seq", "head"), None),
        check_vma=False,
    )
```

time: 243 us -> 55.8 us (0.23)
  waiting for transfers between devices: 182 us -> 0 us
  Pallas kernels: 0 us -> 52.5 us
  matrix products: 16.5 us -> 0 us
  between operations: 13.7 us -> 0.01 us
  local copies, waits for them, and re-layouts: 13.7 us -> 2.26 us
  other arithmetic: 9.48 us -> 0 us
  starting transfers between devices: 7.03 us -> 0 us
    psum x2 -> x0, waiting for transfers between devices: 175 us -> none  [body(): summed = lax.psum(gradients_now, 'seq')]
    pallas_call x0 -> x1, Pallas kernels: none -> 52.5 us  [body(): pl.pallas_call(functools.partial(kernel, cfg), out_shape=jax.ShapeDtypeSt...]
    dot_general x16 -> x0, matrix products: 16.5 us -> none  [the longest x2 4.54 us: apply_weights(): jnp.einsum('the,hef->thf', hidden_query, applied[2], preferred_element_ty...]
    all_to_all x2 -> x0, waiting for transfers between devices: 7.03 us -> none  [body(): lax.all_to_all(result, 'head', split_axis=0, concat_axis=1, tiled=True)]
    all_to_all x2 -> x0, starting transfers between devices: 6.98 us -> none  [body(): lax.all_to_all(result, 'head', split_axis=0, concat_axis=1, tiled=True)]
    unnamed x31 -> x1, local copies, waits for them, and re-layouts: 9.11 us -> 2.26 us
    reduce_sum x4 -> x0, other arithmetic: 4.65 us -> none  [the longest x2 3.51 us: body(): jnp.mean(summed * summed, axis=(2, 3), keepdims=True) + eps_grad]
    another operation x3 -> x0, other arithmetic: 3.56 us -> none  [the longest x2 2.5 us: gradients(): return jnp.stack([grad_gate, grad_up, grad_down])]
  transfers between devices with their start and end apart: 4 -> 0, of which waited for: 3 -> 0; matrix products, arithmetic and copies ran while one was open for 7% -> 0% of each run, Pallas kernels for 0% -> 0%
where the time goes in v2:
time: 55.8 us; the launch traced here: 54.8 us
  Pallas kernels  52.5 us (94%)
  local copies, waits for them, and re-layouts  2.26 us (4%)
    pallas_call x1, Pallas kernels, body(): pl.pallas_call(functools.partial(kernel, cfg), out_shape=jax.ShapeDtypeSt...  52.5 us
    unnamed x1, local copies, waits for them, and re-layouts  2.26 us

profile of v2, /device:TPU:0, one launch (start us, length us, event | category | flops | bytes accessed | tf_op | source)
XLA Modules:
  0.0 54.8 jit_solution(3208979482534604403)
XLA Ops:
  0.0 52.5 %shard_map.55 = bf16[2,256,1024]{2,1,0:T(8,128)(2,1)} custom-call(bf16[2,512,512]{2,1,0:T(8,128)(2,1)} %q_hbm.1, bf16[2,512,512]{2,1,0:T(8,128)(2,1)} %k_hbm.1, bf16[2,512,512]{2,1,0:T(8,128)(2,1)} %v_hbm.1, f32[3,2,2,512]{3,2,1,0:T(2,128)} %rates.1, bf16[3,2,256,256]{3,2,1,0:T(8,128)(2,1)} %w_hbm.1), custom_call_target="tpu_custom_call" | custom-call | tf_op jit(solution)/shard_map/pallas_call | solution.py:360
  52.6 2.3 %copy.7 = bf16[2,256,1024]{2,1,0:T(8,128)(2,1)} copy(bf16[2,256,1024]{2,1,0:T(8,128)(2,1)} %shard_map.55) | data formatting | bytes 2097152

commit v3 on v2

--- a/solution.py
+++ b/solution.py
@@ -34,9 +34,10 @@
 
 def kernel(cfg, q_hbm, k_hbm, v_hbm, rates, w_hbm, out, qb, kb, vb, wb, wf, tgt, lb, lr, rt, ab, bb, ob, load_sem, xs, xr, ss, rs,
            oss, ors, own_sem, *chunk_refs):
-    blocks, heads, tokens, width, tile, ncore, nmid, nhi, nhead = cfg
+    blocks, heads, tokens, width, tile, ncore, nmid, nhi, nhead, subs = cfg
     own = heads // ncore
-    folds = width // lanes
+    folds = width // lanes // subs
+    parts = 3 * subs
     me = lax.axis_index("seq")
     y = lax.axis_index("head")
     core = lax.rem(me, ncore)
@@ -126,13 +127,13 @@
     refs = {}
     for b in range(blocks):
         for h in range(own):
-            for m in range(3):
-                i = (h * 3 + m) * 7
+            for m in range(parts):
+                i = (h * parts + m) * 7
                 refs[b, h, m] = [r.at[b] for r in chunk_refs[i:i + 7]]
 
     def sides(m):
         one, two = (nmid, mid, mid_peers, mid_id), (nhi, hi, hi_peers, hi_id)
-        return (one, two) if m < 2 else (two, one)
+        return (one, two) if m < 3 * subs - subs // 2 else (two, one)
 
     pending = {}
 
@@ -141,7 +142,7 @@
         copies = []
         for d, p in enumerate(peers):
             src, dst = pairs(d, p)
-            sem = ((b * own + h) * 3 + m) * per_chunk + number + d
+            sem = ((b * own + h) * parts + m) * per_chunk + number + d
             copy = pltpu.make_async_remote_copy(src_ref=src, dst_ref=dst, send_sem=ss.at[sem], recv_sem=rs.at[sem],
                                                 device_id=id_of(p), device_id_type=MESH)
             copy.start()
@@ -156,7 +157,9 @@
     def start_first(key, value):
         gf, gb, r1, sf, sb, r2, ag = refs[key]
         (n1, _, peers, id_of), _ = sides(key[2])
-        folded = jnp.concatenate([value[:, j * lanes:(j + 1) * lanes] for j in range(folds)], axis=0).reshape(gf.shape)
+        first = key[2] % subs * folds
+        folded = [value[:, j * lanes:(j + 1) * lanes] for j in range(first, first + folds)]
+        folded = jnp.concatenate(folded, axis=0).reshape(gf.shape)
         gf[...] = folded
         gb[...] = folded.astype(BF16)
         exchange(key, 0, lambda d, p: (gb.at[p], r1.at[d]), peers, id_of)
@@ -191,10 +194,14 @@
         exchange(key, n1 + 2 * n2 - 3, lambda d, p: (part, part), peers, id_of)
 
     def update(key):
-        finish(key)
         b, h, m = key
-        x = refs[key][6][...].reshape(folds * width, lanes)
-        n = jnp.concatenate([x[j * width:(j + 1) * width].astype(F32) for j in range(folds)], axis=1)
+        n = []
+        for j in range(subs):
+            part = (b, h, m * subs + j)
+            finish(part)
+            x = refs[part][6][...].reshape(folds * width, lanes)
+            n += [x[i * width:(i + 1) * width].astype(F32) for i in range(folds)]
+        n = jnp.concatenate(n, axis=1)
         mean = jnp.sum(jnp.sum(n * n, axis=0, keepdims=True), axis=1, keepdims=True) * (1.0 / (width * width))
         stepped = wf[h, m] + n * (step_size * lax.rsqrt(mean + eps_grad))
         new = stepped * (tgt[h, m] * lax.rsqrt(jnp.mean(stepped * stepped, axis=-1, keepdims=True) + eps_row))
@@ -242,10 +249,13 @@
                         rt[lax.rem(core + ncore - 1 - e, ncore)] = jnp.transpose(lr[e])
             part(p)
         flat = ncore * tokens
-        start_first((b, h, 2), dot(ab[...].reshape(flat, width), vb[b, :, :, cols].reshape(flat, width), 0, 0))
+        n2 = dot(ab[...].reshape(flat, width), vb[b, :, :, cols].reshape(flat, width), 0, 0)
+        for j in range(subs):
+            start_first((b, h, 2 * subs + j), n2)
         n13 = dot(kb[b, :, :, cols].reshape(flat, width), bb[...].reshape(flat, 2 * width), 0, 0)
-        start_first((b, h, 0), n13[:, :width])
-        start_first((b, h, 1), n13[:, width:])
+        for m in range(2):
+            for j in range(subs):
+                start_first((b, h, m * subs + j), n13[:, m * width:(m + 1) * width])
 
     part_tokens = tokens // nhead
     out_copies = []
@@ -283,7 +293,7 @@
         grads(0, h)
     for b in range(blocks):
         turn = (2, 0, 1)
-        keys = [(b, h, m) for h in range(own) for m in turn]
+        keys = [(b, h, m * subs + j) for h in range(own) for m in turn for j in range(subs)]
         for key in keys:
             start_second(key)
         if b:
@@ -297,8 +307,9 @@
                     update((b, h, m))
                 grads(b + 1, h)
         else:
-            for key in keys:
-                update(key)
+            for h in range(own):
+                for m in turn:
+                    update((b, h, m))
             apply(b)
 
     for copy in out_copies:
@@ -318,13 +329,16 @@
         ncore, nmid, nhi = split_of(nseq, heads)
         own = heads // ncore
         tile = 128 if tokens % 128 == 0 else tokens
-        cfg = (blocks, heads, tokens, width, tile, ncore, nmid, nhi, nhead)
+        folds = width // lanes
+        share = nmid * nhi
+        subs = next(n for n in range(folds, 0, -1) if folds % n == 0 and (folds // n * width % (16 * share) == 0 or n == 1))
+        cfg = (blocks, heads, tokens, width, tile, ncore, nmid, nhi, nhead, subs)
         vmem = pltpu.VMEM
         dma = pltpu.SemaphoreType.DMA
         loads = 3 * blocks
         others = max(ncore - 1, 1)
         lines = -(-3 * blocks * own // 8) * 8
-        copies = blocks * own * 3 * 2 * (nmid - 1 + nhi - 1)
+        copies = blocks * own * 3 * subs * 2 * (nmid - 1 + nhi - 1)
         out_copies = blocks * (ncore * nhead - 1)
         scratch = [
             *[vmem((blocks, ncore, tokens, own * width), BF16)] * 3,
@@ -343,10 +357,10 @@
             *[dma((out_copies,))] * 2,
             dma((blocks,)),
         ]
-        piece = width * width // lanes // (nmid * nhi)
+        piece = width * folds // subs // share
         for _ in range(own):
-            for m in range(3):
-                n1, n2 = (nmid, nhi) if m < 2 else (nhi, nmid)
+            for m in range(3 * subs):
+                n1, n2 = (nmid, nhi) if m < 3 * subs - subs // 2 else (nhi, nmid)
                 scratch += [
                     vmem((blocks, n1, n2, piece, lanes), F32),
                     vmem((blocks, n1, n2, piece, lanes), BF16),

time: 55.8 us -> 53.3 us (0.955)
  Pallas kernels: 52.5 us -> 50.1 us
    pallas_call x1, Pallas kernels: 52.5 us -> 50.1 us  [body(): pl.pallas_call(functools.partial(kernel, cfg), out_shape=jax.ShapeDtypeSt...]
where the time goes in v3:
time: 53.3 us; the launch traced here: 52.3 us
  Pallas kernels  50.1 us (94%)
  local copies, waits for them, and re-layouts  2.26 us (4%)
    pallas_call x1, Pallas kernels, body(): pl.pallas_call(functools.partial(kernel, cfg), out_shape=jax.ShapeDtypeSt...  50.1 us
    unnamed x1, local copies, waits for them, and re-layouts  2.26 us

profile of v3, /device:TPU:0, one launch (start us, length us, event | category | flops | bytes accessed | tf_op | source)
XLA Modules:
  0.0 52.3 jit_solution(18338267955426177990)
XLA Ops:
  0.0 50.1 %shard_map.55 = bf16[2,256,1024]{2,1,0:T(8,128)(2,1)} custom-call(bf16[2,512,512]{2,1,0:T(8,128)(2,1)} %q_hbm.1, bf16[2,512,512]{2,1,0:T(8,128)(2,1)} %k_hbm.1, bf16[2,512,512]{2,1,0:T(8,128)(2,1)} %v_hbm.1, f32[3,2,2,512]{3,2,1,0:T(2,128)} %rates.1, bf16[3,2,256,256]{3,2,1,0:T(8,128)(2,1)} %w_hbm.1), custom_call_target="tpu_custom_call" | custom-call | tf_op jit(solution)/shard_map/pallas_call | solution.py:374
  50.1 2.3 %copy.7 = bf16[2,256,1024]{2,1,0:T(8,128)(2,1)} copy(bf16[2,256,1024]{2,1,0:T(8,128)(2,1)} %shard_map.55) | data formatting | bytes 2097152

commit v4 on v3

--- a/solution.py
+++ b/solution.py
@@ -296,11 +296,12 @@
         keys = [(b, h, m * subs + j) for h in range(own) for m in turn for j in range(subs)]
         for key in keys:
             start_second(key)
+        for key in keys:
+            start_third(key)
         if b:
             apply(b - 1)
-        for step in (start_third, start_fourth):
-            for key in keys:
-                step(key)
+        for key in keys:
+            start_fourth(key)
         if b < blocks - 1:
             for h in range(own):
                 for m in turn:

time: 53.3 us -> 52.8 us (level)
  Pallas kernels: 50.1 us -> 49.5 us
where the time goes in v4:
time: 52.8 us; the launch traced here: 51.8 us
  Pallas kernels  49.5 us (94%)
  local copies, waits for them, and re-layouts  2.26 us (4%)
    pallas_call x1, Pallas kernels, body(): pl.pallas_call(functools.partial(kernel, cfg), out_shape=jax.ShapeDtypeSt...  49.5 us
    unnamed x1, local copies, waits for them, and re-layouts  2.26 us

profile of v4, /device:TPU:0, one launch (start us, length us, event | category | flops | bytes accessed | tf_op | source)
XLA Modules:
  0.0 51.8 jit_solution(17800258747815678250)
XLA Ops:
  0.0 49.5 %shard_map.55 = bf16[2,256,1024]{2,1,0:T(8,128)(2,1)} custom-call(bf16[2,512,512]{2,1,0:T(8,128)(2,1)} %q_hbm.1, bf16[2,512,512]{2,1,0:T(8,128)(2,1)} %k_hbm.1, bf16[2,512,512]{2,1,0:T(8,128)(2,1)} %v_hbm.1, f32[3,2,2,512]{3,2,1,0:T(2,128)} %rates.1, bf16[3,2,256,256]{3,2,1,0:T(8,128)(2,1)} %w_hbm.1), custom_call_target="tpu_custom_call" | custom-call | tf_op jit(solution)/shard_map/pallas_call | solution.py:375
  49.6 2.3 %copy.7 = bf16[2,256,1024]{2,1,0:T(8,128)(2,1)} copy(bf16[2,256,1024]{2,1,0:T(8,128)(2,1)} %shard_map.55) | data formatting | bytes 2097152
